TPU v7x, 32 devices: a whole 2x2x4 slice. The times are simulated.
32 devices in a mesh: aux: 8 (over z, x), pair: 4 (over y, core).
Axes of the slice: x: 2, y: 2, z: 4, core: 2. Of those that a mesh axis runs over, the one named last changes fastest.
Arguments:
- three_centre: bfloat16 [16, 160, 128, 128], P('pair', 'aux'), may hold values from -6 to 6
- block_mask: int32 [16], replicated, may hold values from 0 to 1, as said below
- block_owner: int32 [16], replicated, may hold values from 0 to 3, as said below
- block_index: int32 [2, 16], replicated, may hold values from 0 to 23
- active_orbitals: bfloat16 [24, 3072], replicated, may hold values from -0.5 to 0.5
- inactive_orbitals: bfloat16 [256, 3072], replicated, may hold values from -0.75 to 0.75
Outputs:
- fock_blocks: float32 [32, 128, 128], P('pair')
- active_integrals: float32 [576, 576], P('aux')
Inputs may be any that keep to these rules, and one draw needn't show every extreme that they name: `block_mask`: every index of pair holds at least 2 live slots. `block_owner`: among the 4 slots of one index of pair, live or not, at most 2 name any one owner; one owner is named by exactly 2 live slots of every index of pair, so it receives 8 live blocks.
All inputs are finite; a program needn't handle non-finite values.
Results may differ from a plain program's by a relative error of at most 0.0044.
Values may be sent and summed in bfloat16 or wider, within the bound.
A program may use at most 64 MiB of HBM per device.

v0:
```python
import math

import jax
import jax.numpy as jnp
from jax import lax
from jax.sharding import PartitionSpec as P


def owner_tables(block_mask, block_owner, slot_count, pair_count):
    owners = jnp.arange(pair_count, dtype=jnp.int32)
    flagged = ((block_owner[:, None] == owners[None, :]) & (block_mask[:, None] == 1)).astype(
        jnp.int32
    )
    global_rank = jnp.sum((jnp.cumsum(flagged, axis=0) - flagged) * flagged, axis=1)
    per_source = flagged.reshape(pair_count, slot_count, pair_count)
    source_rank = jnp.sum((jnp.cumsum(per_source, axis=1) - per_source) * per_source, axis=2)
    slot_places = jnp.arange(slot_count // 2, dtype=jnp.int32)
    matches = (source_rank[:, None, None, :] == slot_places[None, None, :, None]).astype(jnp.int32)
    chosen = jnp.transpose(per_source, (0, 2, 1))[:, :, None, :] * matches
    return (global_rank, chosen)


def slot_pick(route_table, slot_count):
    positions = jnp.arange(slot_count, dtype=jnp.int32)
    return (jnp.sum(route_table * positions, axis=-1), jnp.sum(route_table, axis=-1))


def fitted_terms(blocks, living, row_blocks, col_blocks, active_split, inactive_split, block_width):
    active_rows = jnp.take(active_split, row_blocks, axis=1)
    active_cols = jnp.take(active_split, col_blocks, axis=1)
    half_done = jnp.einsum(
        "rpab,urb->rpua", blocks, active_cols, preferred_element_type=jnp.float32
    ).astype(jnp.bfloat16)
    weighted = active_rows * living.astype(jnp.bfloat16)[None, :, None]
    fitted = jnp.einsum("rpua,tra->ptu", half_done, weighted, preferred_element_type=jnp.float32)
    inactive_rows = jnp.take(inactive_split, row_blocks, axis=1)
    inactive_cols = jnp.take(inactive_split, col_blocks, axis=1)
    density = jnp.einsum(
        "kra,krb->rab", inactive_rows, inactive_cols, preferred_element_type=jnp.float32
    ).astype(jnp.bfloat16)
    density = density * living.astype(jnp.bfloat16)[:, None, None]
    coupling = (
        jnp.einsum("rpab,rab->p", blocks, density, preferred_element_type=jnp.float32) / block_width
    )
    return (fitted.reshape(fitted.shape[0], -1), coupling)


def shards(three_centre, block_mask, block_owner, block_index, active_orbitals, inactive_orbitals):
    slot_count = three_centre.shape[0]
    aux_rows = three_centre.shape[1]
    block_width = three_centre.shape[2]
    pair_count = lax.axis_size("pair")
    aux_count = lax.axis_size("aux")
    total_aux = aux_count * aux_rows
    pair_here = lax.axis_index("pair")
    capacity = slot_count // 2
    active_split = active_orbitals.reshape(active_orbitals.shape[0], -1, block_width)
    inactive_split = inactive_orbitals.reshape(inactive_orbitals.shape[0], -1, block_width)
    global_rank, chosen = owner_tables(block_mask, block_owner, slot_count, pair_count)
    outgoing = jnp.take(chosen, pair_here, axis=0)
    incoming = jnp.take(chosen, pair_here, axis=1)
    send_slot, send_live = slot_pick(outgoing, slot_count)
    recv_slot, recv_live = slot_pick(incoming, slot_count)
    source_starts = jnp.arange(pair_count, dtype=jnp.int32)[:, None] * slot_count
    recv_global = (source_starts + recv_slot).reshape(-1)
    recv_live = recv_live.reshape(-1)
    send_flat = send_slot.reshape(-1)
    send_mask = send_live.reshape(-1)
    block_slots = pair_here * slot_count + jnp.arange(slot_count, dtype=jnp.int32)
    living = jnp.take(block_mask, block_slots)
    row_blocks = jnp.take(block_index[0], block_slots)
    col_blocks = jnp.take(block_index[1], block_slots)
    fitted_part, coupling_part = fitted_terms(
        three_centre, living, row_blocks, col_blocks, active_split, inactive_split, block_width
    )
    fitted_sum, coupling_sum = lax.psum((fitted_part, coupling_part), "pair")
    fitted = fitted_sum.astype(jnp.bfloat16)
    coupling = coupling_sum.astype(jnp.bfloat16)
    coulomb = jnp.einsum(
        "rpab,p->rab", three_centre, coupling, preferred_element_type=jnp.float32
    ) * (1.0 / math.sqrt(total_aux))
    outbound = jnp.take(coulomb, send_flat, axis=0) * send_mask.astype(jnp.float32)[:, None, None]
    outbound = outbound.reshape(pair_count, capacity, block_width, block_width)
    coulomb = lax.all_to_all(outbound, "pair", split_axis=0, concat_axis=0, tiled=True).reshape(
        pair_count * capacity, block_width, block_width
    )
    slot_rank = jnp.take(global_rank, recv_global)
    owned_slots = pair_count * capacity
    rank_values = jnp.arange(owned_slots, dtype=jnp.int32)
    selector = (slot_rank[None, :] == rank_values[:, None]).astype(jnp.float32) * recv_live.astype(
        jnp.float32
    )[None, :]
    fock_part = jnp.einsum("kr,rab->kab", selector, coulomb, precision=lax.Precision.HIGHEST)
    fock_blocks = lax.psum(fock_part, "aux")
    partial_terms = jnp.dot(fitted.T, fitted, preferred_element_type=jnp.float32)
    gram_block = lax.psum_scatter(partial_terms, "aux", scatter_dimension=0, tiled=True) / total_aux
    return (fock_blocks, gram_block)


def solution(mesh):
    return jax.shard_map(
        shards,
        mesh=mesh,
        in_specs=(P("pair", "aux", None, None), P(), P(), P(), P(), P()),
        out_specs=(P("pair", None, None), P("aux", None)),
        check_vma=False,
    )
```

profile of v0, /device:TPU:0, one launch (start us, length us, event | category | flops | bytes accessed | tf_op | source)
XLA Modules:
  0.0 204.8 jit_solution(16277229511183143157)
XLA Ops:
  7.2 2.8 %copy.30 = bf16[256,3072]{0,1:T(8,128)(2,1)} copy(bf16[256,3072]{1,0:T(8,128)(2,1)} %param.17) | data formatting | bytes 3145728 | tf_op args[5]
  10.0 2.6 %copy.31 = bf16[256,24,128]{2,0,1:T(8,128)(2,1)} copy(bf16[256,24,128]{0,2,1:T(8,128)(2,1)} %bitcast.78) | data formatting | bytes 3145728 | tf_op jit(solution)/shard_map/reshape | solution.py:58
  12.6 0.6 gather_fusion.4
  13.2 0.6 gather_fusion.2
  13.9 2.0 gather_fusion.5
  15.9 2.0 gather_fusion.3
  18.0 0.6 gather_fusion.8
  18.6 0.6 gather_fusion.7
  19.1 0.6 gather_fusion.6
  21.2 3.0 %fusion.23 = f32[20]{0:T(128)S(1)} fusion(bf16[4,20,128,128]{3,2,1,0:T(8,128)(2,1)S(1)} %copy-done, bf16[4,128,128,1]{2,1,0,3:T(8,128)(2,1)S(1)} %fusion.19), kind=kOutput, calls=%fused_computation.23 | convolution fusion | flops 2621460 | bytes 2752592 | tf_op jit(solution)/shard_map/rpab,rab->p/dot_general | solution.py:43
  24.2 1.9 fusion.15
  26.2 13.5 %all-reduce.1 = (bf16[20]{0:T(256)(128)(2,1)S(1)}, bf16[20,576]{1,0:T(8,128)(2,1)S(1)}) all-reduce(f32[20]{0:T(128)S(1)} %fusion.23, f32[20,576]{1,0:T(8,128)S(1)} %reshape.182), channel_id=1, replica_groups=mesh['aux'=8,'pair'=4] {'pair'}, use_global_device_ids=true, to_apply=%region_7.10 | all-reduce | flops 11540 | bytes 69240 | tf_op jit(solution)/shard_map/psum | solution.py:76
  39.7 2.1 %fusion = f32[1,4,128,128]{3,0,2,1:T(1,128)S(1)} fusion(bf16[4,20,128,128]{3,2,1,0:T(8,128)(2,1)S(1)} %copy-done, bf16[20]{0:T(256)(128)(2,1)S(1)} %get-tuple-element.39), kind=kOutput, calls=%fused_computation.9 | convolution fusion | flops 2621440 | bytes 2883624 | tf_op jit(solution)/shard_map/rpab,p->rab/dot_general | solution.py:79
  42.0 0.6 gather_fusion.1
  42.6 1.3 fusion.26
  44.0 3.5 %all-to-all-start = ((f32[4,2,128,128]{3,1,2,0:T(2,128)}), f32[4,2,128,128]{3,1,2,0:T(2,128)S(1)}, u32[]{:S(2)}, u32[]{:S(2)}) async-start(f32[4,2,128,128]{3,1,2,0:T(2,128)} %fusion.26), calls=%async_computation | async-start | bytes 1048576 | tf_op jit(solution)/shard_map/all_to_all | solution.py:84
  48.1 0.7 gather_fusion
  48.8 7.5 %all-to-all-done = f32[4,2,128,128]{3,1,2,0:T(2,128)S(1)} async-done(((f32[4,2,128,128]{3,1,2,0:T(2,128)}), f32[4,2,128,128]{3,1,2,0:T(2,128)S(1)}, u32[]{:S(2)}, u32[]{:S(2)}) %all-to-all-start) | async-done | bytes 524320 | tf_op jit(solution)/shard_map/all_to_all | solution.py:84
  56.4 1.4 fusion.56
  57.9 1.5 fusion.73
  59.4 71.2 %all-reduce.4.cloned.1.call-done = f32[8,128,128]{2,0,1:T(8,128)} async-done(((f32[8,128,128]{2,0,1:T(8,128)}), f32[8,128,128]{2,0,1:T(8,128)}) %all-reduce.4.cloned.1.call-update) | async-done | bytes 524304 | tf_op jit(solution)/shard_map/psum | solution.py:94
  130.6 1.9 copy.39
  132.6 63.8 %reduce-scatter.4.cloned.1.call-done = f32[72,576]{1,0:T(8,128)} async-done(((f32[576,576]{1,0:T(8,128)}), f32[72,576]{1,0:T(8,128)}) %reduce-scatter.4.cloned.1.call-update) | async-done | bytes 165904
  196.4 1.6 broadcast_multiply_fusion.1
  (53 shorter events, 2.7 us)
Async XLA Ops:
  7.2 14.0 %copy-start = (bf16[4,20,128,128]{3,2,1,0:T(8,128)(2,1)S(1)}, bf16[4,20,128,128]{3,2,1,0:T(8,128)(2,1)}, u32[]{:S(2)}) copy-start(bf16[4,20,128,128]{3,2,1,0:T(8,128)(2,1)} %param.12) | copy-start | bytes 7864324
  7.2 5.4 %copy-start.4 = (s32[2,16]{1,0:T(2,128)S(1)}, s32[2,16]{1,0:T(2,128)}, u32[]{:S(2)}) copy-start(s32[2,16]{1,0:T(2,128)} %param.15) | copy-start | bytes 388
  9.9 8.0 %copy-start.2 = (bf16[24,3072]{1,0:T(8,128)(2,1)S(1)}, bf16[24,3072]{1,0:T(8,128)(2,1)}, u32[]{:S(2)}) copy-start(bf16[24,3072]{1,0:T(8,128)(2,1)} %param.16) | copy-start | bytes 442372
  9.9 9.2 %copy-start.1 = (s32[16]{0:T(128)S(1)}, s32[16]{0:T(128)}, u32[]{:S(2)}) copy-start(s32[16]{0:T(128)} %param.13) | copy-start | bytes 196
  10.0 9.8 %copy-start.3 = (s32[16]{0:T(128)S(1)}, s32[16]{0:T(128)}, u32[]{:S(2)}) copy-start(s32[16]{0:T(128)} %param.14) | copy-start | bytes 196
  44.0 12.3 %all-to-all-start = ((f32[4,2,128,128]{3,1,2,0:T(2,128)}), f32[4,2,128,128]{3,1,2,0:T(2,128)S(1)}, u32[]{:S(2)}, u32[]{:S(2)}) async-start(f32[4,2,128,128]{3,1,2,0:T(2,128)} %fusion.26), calls=%async_computation | async-start | bytes 1048576 | tf_op jit(solution)/shard_map/all_to_all | solution.py:84
  47.4 83.2 %all-reduce.4.cloned.1.call-start = ((), (), s32[]{:S(2)}) async-start(), calls=%async_computation.2 | async-start | bytes 1048576 | tf_op jit(solution)/shard_map/psum | solution.py:94
  57.8 138.6 %reduce-scatter.4.cloned.1.call-start = ((), (), s32[]{:S(2)}) async-start(), calls=%async_computation.3 | async-start | bytes 1658880
Sparse Core Ops, SparseCore 0:
  57.9 72.6 all-reduce.3
  134.5 61.8 reduce-scatter.3
where the time goes:
time: 205 us
  waiting for transfers between devices  143 us (70%)
  local copies, waits for them, and re-layouts  16.5 us (8%)
  between operations  14.3 us (7%)
  blocking collectives  13.5 us (7%)
  matrix products  10.2 us (5%)
  other arithmetic  4.29 us (2%)
  starting transfers between devices  3.55 us (2%)
    psum x1, waiting for transfers between devices, shards(): fock_blocks = lax.psum(fock_part, 'aux')  71.2 us
    unnamed x3, waiting for transfers between devices  63.9 us
    psum x1, blocking collectives, shards(): fitted_sum, coupling_sum = lax.psum((fitted_part, coupling_part), 'pair')  13.5 us
    all_to_all x1, waiting for transfers between devices, shards(): lax.all_to_all(outbound, 'pair', split_axis=0, concat_axis=0, tiled=True)  7.47 us
    unnamed x12, local copies, waits for them, and re-layouts  4.71 us
  transfers between devices with their start and end apart: 3, of which 3 were waited for; matrix products, arithmetic and copies ran while one was open for 2% of the time, Pallas kernels for 0%

commit v1 on v0

v1 whole, which is shorter than its diff:
```python
import functools
import math

import jax
import jax.numpy as jnp
from jax import lax
from jax.experimental import pallas as pl
from jax.experimental.pallas import tpu as pltpu
from jax.sharding import PartitionSpec as P

F32 = jnp.float32
BF16 = jnp.bfloat16
NT = (((1,), (1,)), ((), ()))
TN = (((0,), (0,)), ((), ()))


def remote(src, dst, send_sem, recv_sem, axis, peer):
    return pltpu.make_async_remote_copy(
        src_ref=src,
        dst_ref=dst,
        send_sem=send_sem,
        recv_sem=recv_sem,
        device_id={axis: peer},
        device_id_type=pl.DeviceIdType.MESH,
    )


def peers_of(me, count):
    return [lax.rem(me + off, count) for off in range(1, count)]


def kernel(
    n_aux,
    n_pair,
    three_hbm,
    mask_s,
    owner_s,
    index_s,
    act_v,
    inact_hbm,
    fock_o,
    gram_o,
    t_v,
    inact_v,
    act_blocks,
    coup_acc,
    coup_all,
    coup_rows,
    half_v,
    aexp_v,
    fit_part,
    fit_all,
    fit_full,
    coul_send,
    coul_recv,
    red_all,
    fock_all,
    t_sem,
    in_sem,
    c_send,
    c_recv,
    f_send,
    f_recv,
    r_send,
    r_recv,
    g_send,
    g_recv,
    m_send,
    m_recv,
    p_send,
    p_recv,
    a_send,
    a_recv,
):
    slots, rows, width = t_v.shape[0], t_v.shape[1], t_v.shape[2]
    act = act_v.shape[0]
    act_pad = half_v.shape[1]
    pairs = act * act
    chunks, chunk_rows = coul_send.shape[0], coul_send.shape[2]
    parts = fit_part.shape[0]
    part_rows = rows // parts
    owned = fock_o.shape[0]
    gram_rows = gram_o.shape[0]
    total_aux = n_aux * rows
    me_a = lax.axis_index("aux")
    me_p = lax.axis_index("pair")
    my_part = lax.rem(me_p, parts)
    mate = me_p + 1 - 2 * my_part
    aux_peers = peers_of(me_a, n_aux)
    pair_peers = peers_of(me_p, n_pair)
    reducer = me_a < chunks

    def if_reducer(body):
        if chunks == n_aux:
            body()
        else:
            pl.when(reducer)(body)

    blocks = inact_v.shape[0]
    inact_copies = [
        pltpu.make_async_copy(
            inact_hbm.at[:, n * width : (n + 1) * width], inact_v.at[n], in_sem.at[n]
        )
        for n in range(blocks)
    ]
    for copy in inact_copies:
        copy.start()
    t_copies = [
        pltpu.make_async_copy(three_hbm.at[g], t_v.at[g], t_sem.at[g]) for g in range(slots)
    ]
    for copy in t_copies:
        copy.start()

    barrier = pltpu.get_barrier_semaphore()
    for peer in aux_peers:
        pl.semaphore_signal(
            barrier, inc=1, device_id={"aux": peer}, device_id_type=pl.DeviceIdType.MESH
        )
    for peer in pair_peers:
        pl.semaphore_signal(
            barrier, inc=1, device_id={"pair": peer}, device_id_type=pl.DeviceIdType.MESH
        )

    base = me_p * slots
    living = [mask_s[base + g] for g in range(slots)]
    row_at = [index_s[0, base + g] for g in range(slots)]
    col_at = [index_s[1, base + g] for g in range(slots)]
    for n in range(blocks):
        act_blocks[n] = act_v[:, n * width : (n + 1) * width].astype(F32)

    first = lax.broadcasted_iota(jnp.int32, (pairs, act), 0) // act
    spread = (first == lax.broadcasted_iota(jnp.int32, (pairs, act), 1)).astype(BF16)
    for g in range(slots):
        rows_g = act_blocks[row_at[g]] * living[g].astype(F32)
        aexp_v[:, g * width : (g + 1) * width] = jnp.dot(
            spread, rows_g.astype(BF16), preferred_element_type=F32
        ).astype(BF16)

    for copy in inact_copies:
        copy.wait()
    step = math.gcd(rows, 4)
    for g in range(slots):
        density = lax.dot_general(
            inact_v[row_at[g]],
            inact_v[col_at[g]],
            TN,
            preferred_element_type=F32,
        )
        density = density.astype(BF16).astype(F32) * living[g].astype(F32)
        t_copies[g].wait()

        def coupling_step(i, carry, g=g, density=density):
            for j in range(step):
                p = i * step + j
                prod = t_v[g, p].astype(F32) * density
                part = jnp.sum(prod.reshape(width // 8, 8, width), axis=0)
                if g > 0:
                    part = part + coup_acc[p]
                coup_acc[p] = part
            return carry

        lax.fori_loop(0, rows // step, coupling_step, 0)
    coup_all[me_p] = jnp.sum(coup_acc[...], axis=1)

    pl.semaphore_wait(barrier, n_aux + n_pair - 2)
    coup_copies = [
        remote(coup_all.at[me_p], coup_all.at[me_p], c_send.at[i], c_recv.at[me_p], "pair", peer)
        for i, peer in enumerate(pair_peers)
    ]
    for copy in coup_copies:
        copy.start()

    zeros = jnp.zeros((act_pad - act, width), F32)
    for g in range(slots):
        cols_g = jnp.concatenate([act_blocks[col_at[g]], zeros], axis=0).astype(BF16)

        def half_step(i, carry, g=g, cols_g=cols_g):
            block = t_v[g, pl.ds(i * step, step)].reshape(step * width, width)
            half = lax.dot_general(cols_g, block, NT, preferred_element_type=F32)
            for j in range(step):
                half_v[i * step + j, :, g * width : (g + 1) * width] = half[
                    :, j * width : (j + 1) * width
                ].astype(BF16)
            return carry

        lax.fori_loop(0, rows // step, half_step, 0)
    second = lax.rem(lax.broadcasted_iota(jnp.int32, (act_pad, pairs), 1), act)
    keep = (second == lax.broadcasted_iota(jnp.int32, (act_pad, pairs), 0)).astype(F32)
    fit_part[...] = jnp.zeros(fit_part.shape, F32)
    for h in range(parts):
        block = half_v[h * part_rows : (h + 1) * part_rows].reshape(part_rows * act_pad, -1)
        full = lax.dot_general(block, aexp_v[...], NT, preferred_element_type=F32)
        full = full.reshape(part_rows, act_pad, pairs) * keep[None]
        fit_part[h, 0:part_rows, :] = jnp.sum(full, axis=1)
    fit_copies = [
        remote(
            fit_part.at[lax.rem(peer, parts)],
            fit_all.at[me_p],
            f_send.at[i],
            f_recv.at[me_p],
            "pair",
            peer,
        )
        for i, peer in enumerate(pair_peers)
    ]
    for copy in fit_copies:
        copy.start()

    for i, peer in enumerate(pair_peers):
        remote(
            coup_all.at[peer], coup_all.at[peer], c_send.at[i], c_recv.at[peer], "pair", peer
        ).wait_recv()
    coupling = jnp.sum(jnp.sum(coup_all[...], axis=0), axis=1, keepdims=True) * (1.0 / width)
    coupling = coupling.astype(BF16).astype(F32)
    coup_rows[...] = jnp.broadcast_to(coupling, coup_rows.shape)
    for g in range(slots):

        def coulomb_step(i, total, g=g):
            for j in range(step):
                p = i * step + j
                total = total + t_v[g, p].astype(F32) * coup_rows[pl.ds(p, 1), :]
            return total

        total = lax.fori_loop(0, rows // step, coulomb_step, jnp.zeros((width, width), F32))
        coul_send[:, g] = total.astype(BF16).reshape(chunks, chunk_rows, width)

    def each_target(body):
        for off in range(chunks):
            if chunks == n_aux:
                if off > 0:
                    body(off, lax.rem(me_a + off, n_aux))
            else:
                pl.when(me_a != off)(functools.partial(body, off, off))

    def start_chunk(i, peer):
        remote(
            coul_send.at[peer], coul_recv.at[me_a], r_send.at[i], r_recv.at[me_a], "aux", peer
        ).start()

    def end_chunk(i, peer):
        remote(
            coul_send.at[peer], coul_recv.at[me_a], r_send.at[i], r_recv.at[me_a], "aux", peer
        ).wait_send()

    each_target(start_chunk)

    for i, peer in enumerate(pair_peers):
        remote(
            fit_part.at[0], fit_all.at[peer], f_send.at[i], f_recv.at[peer], "pair", peer
        ).wait_recv()
    fit_all[me_p] = fit_part[my_part]
    fit_full[my_part, me_a] = jnp.sum(fit_all[...], axis=0).astype(BF16)
    fit_gather = [
        remote(
            fit_full.at[my_part, me_a],
            fit_full.at[my_part, me_a],
            g_send.at[i],
            g_recv.at[me_a],
            "aux",
            peer,
        )
        for i, peer in enumerate(aux_peers)
    ]
    for copy in fit_gather:
        copy.start()

    def reduce_chunk():
        total = coul_send[me_a].astype(F32)
        for i, peer in enumerate(aux_peers):
            remote(
                coul_recv.at[peer], coul_recv.at[peer], r_send.at[0], r_recv.at[peer], "aux", peer
            ).wait_recv()
            total = total + coul_recv[peer].astype(F32)
        red_all[me_p] = (total * (1.0 / math.sqrt(total_aux))).astype(BF16)
        for i, peer in enumerate(pair_peers):
            remote(
                red_all.at[me_p], red_all.at[me_p], p_send.at[i], p_recv.at[me_p], "pair", peer
            ).start()

    if_reducer(reduce_chunk)

    places = []
    count = jnp.int32(0)
    for h in range(n_pair * slots):
        mine = (owner_s[h] == me_p).astype(jnp.int32) * mask_s[h]
        count = count + mine
        places.append(count * mine)

    def place_chunk():
        for i, peer in enumerate(pair_peers):
            remote(
                red_all.at[peer], red_all.at[peer], p_send.at[i], p_recv.at[peer], "pair", peer
            ).wait_recv()
        for k in range(owned):
            block = jnp.zeros((chunk_rows, width), F32)
            for h in range(k, n_pair * slots):
                weight = (places[h] == k + 1).astype(F32)
                block = block + weight * red_all[h // slots, h % slots].astype(F32)
            fock_all[me_a, k] = block.astype(BF16)
        for i, peer in enumerate(aux_peers):
            remote(
                fock_all.at[me_a], fock_all.at[me_a], a_send.at[i], a_recv.at[me_a], "aux", peer
            ).start()
        for k in range(owned):
            fock_o[k, pl.ds(pl.multiple_of(me_a * chunk_rows, chunk_rows), chunk_rows), :] = (
                fock_all[me_a, k].astype(F32)
            )

    if_reducer(place_chunk)

    for i, peer in enumerate(aux_peers):
        remote(
            fit_full.at[my_part, peer],
            fit_full.at[my_part, peer],
            g_send.at[i],
            g_recv.at[peer],
            "aux",
            peer,
        ).wait_recv()
    to_mate = remote(
        fit_full.at[my_part], fit_full.at[my_part], m_send, m_recv, "pair", mate
    )
    to_mate.start()
    remote(
        fit_full.at[1 - my_part], fit_full.at[1 - my_part], m_send, m_recv, "pair", mate
    ).wait_recv()
    fitted = fit_full[...].reshape(-1, pairs)
    picked = lax.broadcasted_iota(jnp.int32, (gram_rows, pairs), 0) + me_a * gram_rows
    pick = (picked == lax.broadcasted_iota(jnp.int32, (gram_rows, pairs), 1)).astype(BF16)
    left = lax.dot_general(pick, fitted, NT, preferred_element_type=F32).astype(BF16)
    gram_o[...] = jnp.dot(left, fitted, preferred_element_type=F32) * (1.0 / total_aux)

    def each_source(body):
        for off in range(chunks):
            if chunks == n_aux:
                if off > 0:
                    body(lax.rem(me_a + off, n_aux))
            else:
                pl.when(me_a != off)(functools.partial(body, off))

    def take_chunk(peer):
        remote(
            fock_all.at[peer], fock_all.at[peer], a_send.at[0], a_recv.at[peer], "aux", peer
        ).wait_recv()
        at = peer * chunk_rows
        if not isinstance(at, int):
            at = pl.multiple_of(at, chunk_rows)
        for k in range(owned):
            fock_o[k, pl.ds(at, chunk_rows), :] = fock_all[peer, k].astype(F32)

    each_source(take_chunk)

    for copy in coup_copies + fit_copies + fit_gather:
        copy.wait_send()
    to_mate.wait_send()
    each_target(end_chunk)

    def end_sends():
        for i, peer in enumerate(pair_peers):
            remote(
                red_all.at[me_p], red_all.at[me_p], p_send.at[i], p_recv.at[me_p], "pair", peer
            ).wait_send()
        for i, peer in enumerate(aux_peers):
            remote(
                fock_all.at[me_a], fock_all.at[me_a], a_send.at[i], a_recv.at[me_a], "aux", peer
            ).wait_send()

    if_reducer(end_sends)


def shards(three_centre, block_mask, block_owner, block_index, active_orbitals, inactive_orbitals):
    slots, rows, width, _ = three_centre.shape
    n_aux = lax.axis_size("aux")
    n_pair = lax.axis_size("pair")
    act = active_orbitals.shape[0]
    blocks = active_orbitals.shape[1] // width
    pairs = act * act
    act_pad = -(-act // 16) * 16
    chunk_rows = max(16, width // n_aux)
    chunks = width // chunk_rows
    parts = 2
    part_pad = -(-(rows // parts) // 16) * 16
    owned = n_pair * slots // 2
    dma = pltpu.SemaphoreType.DMA
    smem = pl.BlockSpec(memory_space=pltpu.SMEM)
    vmem = pl.BlockSpec(memory_space=pltpu.VMEM)
    anywhere = pl.BlockSpec(memory_space=pl.ANY)
    return pl.pallas_call(
        functools.partial(kernel, n_aux, n_pair),
        out_shape=(
            jax.ShapeDtypeStruct((owned, width, width), F32),
            jax.ShapeDtypeStruct((pairs // n_aux, pairs), F32),
        ),
        in_specs=[anywhere, smem, smem, smem, vmem, anywhere],
        out_specs=(vmem, vmem),
        scratch_shapes=[
            pltpu.VMEM(three_centre.shape, BF16),
            pltpu.VMEM((blocks, inactive_orbitals.shape[0], width), BF16),
            pltpu.VMEM((blocks, act, width), F32),
            pltpu.VMEM((rows, 8, width), F32),
            pltpu.VMEM((n_pair, rows, width), F32),
            pltpu.VMEM((rows, width), F32),
            pltpu.VMEM((rows, act_pad, slots * width), BF16),
            pltpu.VMEM((pairs, slots * width), BF16),
            pltpu.VMEM((parts, part_pad, pairs), F32),
            pltpu.VMEM((n_pair, part_pad, pairs), F32),
            pltpu.VMEM((parts, n_aux, part_pad, pairs), BF16),
            pltpu.VMEM((chunks, slots, chunk_rows, width), BF16),
            pltpu.VMEM((n_aux, slots, chunk_rows, width), BF16),
            pltpu.VMEM((n_pair, slots, chunk_rows, width), BF16),
            pltpu.VMEM((chunks, owned, chunk_rows, width), BF16),
            dma((slots,)),
            dma((blocks,)),
            dma((n_pair,)),
            dma((n_pair,)),
            dma((n_pair,)),
            dma((n_pair,)),
            dma((chunks,)),
            dma((n_aux,)),
            dma((n_aux,)),
            dma((n_aux,)),
            dma,
            dma,
            dma((n_pair,)),
            dma((n_pair,)),
            dma((n_aux,)),
            dma((chunks,)),
        ],
        compiler_params=pltpu.CompilerParams(
            collective_id=0, has_side_effects=True, vmem_limit_bytes=48 * 1024 * 1024
        ),
    )(
        three_centre,
        block_mask,
        block_owner,
        block_index,
        active_orbitals,
        inactive_orbitals,
    )


def solution(mesh):
    return jax.shard_map(
        shards,
        mesh=mesh,
        in_specs=(P("pair", "aux", None, None), P(), P(), P(), P(), P()),
        out_specs=(P("pair", None, None), P("aux", None)),
        check_vma=False,
    )
```

time: 205 us -> 35.7 us (0.17)
  waiting for transfers between devices: 143 us -> 0 us
  Pallas kernels: 0 us -> 27 us
  between operations: 14.3 us -> 0.65 us
  blocking collectives: 13.5 us -> 0 us
  matrix products: 10.2 us -> 0 us
  local copies, waits for them, and re-layouts: 16.5 us -> 7.51 us
  other arithmetic: 4.29 us -> 0 us
  starting transfers between devices: 3.55 us -> 0 us
    psum x1 -> x0, waiting for transfers between devices: 71.2 us -> none  [shards(): fock_blocks = lax.psum(fock_part, 'aux')]
    unnamed x3 -> x0, waiting for transfers between devices: 63.9 us -> none
    pallas_call x0 -> x1, Pallas kernels: none -> 27 us  [shards(): pl.pallas_call(functools.partial(kernel, n_aux, n_pair), out_shape=(jax.S...]
    psum x1 -> x0, blocking collectives: 13.5 us -> none  [shards(): fitted_sum, coupling_sum = lax.psum((fitted_part, coupling_part), 'pair')]
    dot_general x6 -> x0, matrix products: 10.2 us -> none  [the longest x1 2.98 us: fitted_terms(): jnp.einsum('rpab,rab->p', blocks, density, preferred_element_type=jnp.flo...]
    gather x9 -> x0, local copies, waits for them, and re-layouts: 8.28 us -> none  [the longest x1 2 us: fitted_terms(): inactive_cols = jnp.take(inactive_split, col_blocks, axis=1)]
    all_to_all x1 -> x0, waiting for transfers between devices: 7.47 us -> none  [shards(): lax.all_to_all(outbound, 'pair', split_axis=0, concat_axis=0, tiled=True)]
    all_to_all x1 -> x0, starting transfers between devices: 3.47 us -> none  [shards(): lax.all_to_all(outbound, 'pair', split_axis=0, concat_axis=0, tiled=True)]
  transfers between devices with their start and end apart: 3 -> 0, of which waited for: 3 -> 0; matrix products, arithmetic and copies ran while one was open for 2% -> 0% of each run, Pallas kernels for 0% -> 0%
where the time goes in v1:
time: 35.7 us; the launch traced here: 35.2 us
  Pallas kernels  27 us (76%)
  local copies, waits for them, and re-layouts  7.51 us (21%)
  between operations  0.65 us (2%)
    pallas_call x1, Pallas kernels, shards(): pl.pallas_call(functools.partial(kernel, n_aux, n_pair), out_shape=(jax.S...  27 us
    unnamed x14, local copies, waits for them, and re-layouts  7.51 us

profile of v1, /device:TPU:0, one launch (start us, length us, event | category | flops | bytes accessed | tf_op | source)
XLA Modules:
  0.0 35.2 jit_solution(9389545560176189567)
XLA Ops:
  0.6 0.0 copy-start
  0.6 1.7 %copy-done = bf16[4,20,128,128]{3,2,1,0:T(8,128)(2,1)S(1)} copy-done((bf16[4,20,128,128]{3,2,1,0:T(8,128)(2,1)S(1)}, bf16[4,20,128,128]{3,2,1,0:T(8,128)(2,1)}, u32[]{:S(2)}) %copy-start) | copy-done | bytes 2621464
  2.4 0.0 copy-start.1
  2.4 1.4 %copy-done.1 = bf16[256,3072]{1,0:T(8,128)(2,1)S(1)} copy-done((bf16[256,3072]{1,0:T(8,128)(2,1)S(1)}, bf16[256,3072]{1,0:T(8,128)(2,1)}, u32[]{:S(2)}) %copy-start.1) | copy-done | bytes 1572888
  3.8 0.0 copy-start.2
  3.8 0.9 %copy-done.2 = bf16[24,3072]{1,0:T(8,128)(2,1)S(1)} copy-done((bf16[24,3072]{1,0:T(8,128)(2,1)S(1)}, bf16[24,3072]{1,0:T(8,128)(2,1)}, u32[]{:S(2)}) %copy-start.2) | copy-done | bytes 147480
  4.7 0.0 copy-start.3
  4.7 0.7 %copy-done.3 = s32[2,16]{1,0:T(2,128)S(1)} copy-done((s32[2,16]{1,0:T(2,128)S(1)}, s32[2,16]{1,0:T(2,128)}, u32[]{:S(2)}) %copy-start.3) | copy-done | bytes 152
  5.4 0.0 copy-start.4
  5.4 0.7 %copy-done.4 = s32[16]{0:T(128)S(1)} copy-done((s32[16]{0:T(128)S(1)}, s32[16]{0:T(128)}, u32[]{:S(2)}) %copy-start.4) | copy-done | bytes 88
  6.0 0.0 copy-start.5
  6.0 0.7 %copy-done.5 = s32[16]{0:T(128)S(1)} copy-done((s32[16]{0:T(128)S(1)}, s32[16]{0:T(128)}, u32[]{:S(2)}) %copy-start.5) | copy-done | bytes 88
  6.7 27.0 %shard_map.77 = (f32[8,128,128]{2,1,0:T(8,128)S(1)}, f32[72,576]{1,0:T(8,128)S(1)}) custom-call(bf16[4,20,128,128]{3,2,1,0:T(8,128)(2,1)S(1)} %copy-done, s32[16]{0:T(128)S(1)} %copy-done.4, s32[16]{0:T(128)S(1)} %copy-done.5, s32[2,16]{1,0:T(2,128)S(1)} %copy-done.3, bf16[24,3072]{1,0:T(8,128)(2,1)S(1)} %copy-done.2, bf16[256,3072]{1,0:T(8,128)(2,1)S(1)} %copy-done.1), custom_call_target="tpu_custom_call" | custom-call | tf_op jit(solution)/shard_map/pallas_call | solution.py:388
  33.7 0.8 %copy.10 = f32[8,128,128]{2,1,0:T(8,128)} copy(f32[8,128,128]{2,1,0:T(8,128)S(1)} %get-tuple-element.4) | data formatting | bytes 1048576
  34.5 0.7 %copy.11 = f32[72,576]{1,0:T(8,128)} copy(f32[72,576]{1,0:T(8,128)S(1)} %get-tuple-element.5) | data formatting | bytes 331776
Async XLA Ops:
  0.6 1.7 %copy-start = (bf16[4,20,128,128]{3,2,1,0:T(8,128)(2,1)S(1)}, bf16[4,20,128,128]{3,2,1,0:T(8,128)(2,1)}, u32[]{:S(2)}) copy-start(bf16[4,20,128,128]{3,2,1,0:T(8,128)(2,1)} %three_hbm.1) | copy-start | bytes 7864324
  2.4 1.4 %copy-start.1 = (bf16[256,3072]{1,0:T(8,128)(2,1)S(1)}, bf16[256,3072]{1,0:T(8,128)(2,1)}, u32[]{:S(2)}) copy-start(bf16[256,3072]{1,0:T(8,128)(2,1)} %inact_hbm.1) | copy-start | bytes 4718596
  3.8 0.9 %copy-start.2 = (bf16[24,3072]{1,0:T(8,128)(2,1)S(1)}, bf16[24,3072]{1,0:T(8,128)(2,1)}, u32[]{:S(2)}) copy-start(bf16[24,3072]{1,0:T(8,128)(2,1)} %act_v.1) | copy-start | bytes 442372
  4.7 0.7 %copy-start.3 = (s32[2,16]{1,0:T(2,128)S(1)}, s32[2,16]{1,0:T(2,128)}, u32[]{:S(2)}) copy-start(s32[2,16]{1,0:T(2,128)} %index_s.1) | copy-start | bytes 388
  5.4 0.7 %copy-start.4 = (s32[16]{0:T(128)S(1)}, s32[16]{0:T(128)}, u32[]{:S(2)}) copy-start(s32[16]{0:T(128)} %mask_s.1) | copy-start | bytes 196
  6.0 0.7 %copy-start.5 = (s32[16]{0:T(128)S(1)}, s32[16]{0:T(128)}, u32[]{:S(2)}) copy-start(s32[16]{0:T(128)} %owner_s.1) | copy-start | bytes 196

commit v2 on v1

--- a/solution.py
+++ b/solution.py
@@ -33,13 +33,17 @@
     n_aux,
     n_pair,
     three_hbm,
+    mask_hbm,
+    owner_hbm,
+    index_hbm,
+    act_hbm,
+    inact_hbm,
+    fock_o,
+    gram_o,
     mask_s,
     owner_s,
     index_s,
     act_v,
-    inact_hbm,
-    fock_o,
-    gram_o,
     t_v,
     inact_v,
     act_blocks,
@@ -55,6 +59,7 @@
     coul_recv,
     red_all,
     fock_all,
+    s_sem,
     t_sem,
     in_sem,
     c_send,
@@ -96,6 +101,14 @@
         else:
             pl.when(reducer)(body)
 
+    small_copies = [
+        pltpu.make_async_copy(source, target, s_sem.at[i])
+        for i, (source, target) in enumerate(
+            [(mask_hbm, mask_s), (owner_hbm, owner_s), (index_hbm, index_s), (act_hbm, act_v)]
+        )
+    ]
+    for copy in small_copies:
+        copy.start()
     blocks = inact_v.shape[0]
     inact_copies = [
         pltpu.make_async_copy(
@@ -121,6 +134,8 @@
             barrier, inc=1, device_id={"pair": peer}, device_id_type=pl.DeviceIdType.MESH
         )
 
+    for copy in small_copies:
+        copy.wait()
     base = me_p * slots
     living = [mask_s[base + g] for g in range(slots)]
     row_at = [index_s[0, base + g] for g in range(slots)]
@@ -135,6 +150,19 @@
         aexp_v[:, g * width : (g + 1) * width] = jnp.dot(
             spread, rows_g.astype(BF16), preferred_element_type=F32
         ).astype(BF16)
+
+    place_at = [jnp.int32(0)] * owned
+    place_on = [jnp.int32(0)] * owned
+    count = jnp.int32(0)
+    for h in range(n_pair * slots):
+        mine = (owner_s[h] == me_p).astype(jnp.int32) * mask_s[h]
+        count = count + mine
+        place = count * mine
+        for k in range(min(owned, h + 1)):
+            hit = (place == k + 1).astype(jnp.int32)
+            place_at[k] = place_at[k] + hit * h
+            place_on[k] = place_on[k] + hit
+    place_on = [on.astype(F32) for on in place_on]
 
     for copy in inact_copies:
         copy.wait()
@@ -184,6 +212,44 @@
             return carry
 
         lax.fori_loop(0, rows // step, half_step, 0)
+    for i, peer in enumerate(pair_peers):
+        remote(
+            coup_all.at[peer], coup_all.at[peer], c_send.at[i], c_recv.at[peer], "pair", peer
+        ).wait_recv()
+    coupling = jnp.sum(jnp.sum(coup_all[...], axis=0), axis=1, keepdims=True) * (1.0 / width)
+    coupling = coupling.astype(BF16).astype(F32)
+    coup_rows[...] = jnp.broadcast_to(coupling, coup_rows.shape)
+    for g in range(slots):
+
+        def coulomb_step(i, total, g=g):
+            for j in range(step):
+                p = i * step + j
+                total = total + t_v[g, p].astype(F32) * coup_rows[pl.ds(p, 1), :]
+            return total
+
+        total = lax.fori_loop(0, rows // step, coulomb_step, jnp.zeros((width, width), F32))
+        coul_send[:, g] = total.astype(BF16).reshape(chunks, chunk_rows, width)
+
+    def each_target(body):
+        for off in range(chunks):
+            if chunks == n_aux:
+                if off > 0:
+                    body(off, lax.rem(me_a + off, n_aux))
+            else:
+                pl.when(me_a != off)(functools.partial(body, off, off))
+
+    def start_chunk(i, peer):
+        remote(
+            coul_send.at[peer], coul_recv.at[me_a], r_send.at[i], r_recv.at[me_a], "aux", peer
+        ).start()
+
+    def end_chunk(i, peer):
+        remote(
+            coul_send.at[peer], coul_recv.at[me_a], r_send.at[i], r_recv.at[me_a], "aux", peer
+        ).wait_send()
+
+    each_target(start_chunk)
+
     second = lax.rem(lax.broadcasted_iota(jnp.int32, (act_pad, pairs), 1), act)
     keep = (second == lax.broadcasted_iota(jnp.int32, (act_pad, pairs), 0)).astype(F32)
     fit_part[...] = jnp.zeros(fit_part.shape, F32)
@@ -206,63 +272,9 @@
     for copy in fit_copies:
         copy.start()
 
-    for i, peer in enumerate(pair_peers):
-        remote(
-            coup_all.at[peer], coup_all.at[peer], c_send.at[i], c_recv.at[peer], "pair", peer
-        ).wait_recv()
-    coupling = jnp.sum(jnp.sum(coup_all[...], axis=0), axis=1, keepdims=True) * (1.0 / width)
-    coupling = coupling.astype(BF16).astype(F32)
-    coup_rows[...] = jnp.broadcast_to(coupling, coup_rows.shape)
-    for g in range(slots):
-
-        def coulomb_step(i, total, g=g):
-            for j in range(step):
-                p = i * step + j
-                total = total + t_v[g, p].astype(F32) * coup_rows[pl.ds(p, 1), :]
-            return total
-
-        total = lax.fori_loop(0, rows // step, coulomb_step, jnp.zeros((width, width), F32))
-        coul_send[:, g] = total.astype(BF16).reshape(chunks, chunk_rows, width)
-
-    def each_target(body):
-        for off in range(chunks):
-            if chunks == n_aux:
-                if off > 0:
-                    body(off, lax.rem(me_a + off, n_aux))
-            else:
-                pl.when(me_a != off)(functools.partial(body, off, off))
-
-    def start_chunk(i, peer):
-        remote(
-            coul_send.at[peer], coul_recv.at[me_a], r_send.at[i], r_recv.at[me_a], "aux", peer
-        ).start()
-
-    def end_chunk(i, peer):
-        remote(
-            coul_send.at[peer], coul_recv.at[me_a], r_send.at[i], r_recv.at[me_a], "aux", peer
-        ).wait_send()
-
-    each_target(start_chunk)
-
-    for i, peer in enumerate(pair_peers):
-        remote(
-            fit_part.at[0], fit_all.at[peer], f_send.at[i], f_recv.at[peer], "pair", peer
-        ).wait_recv()
-    fit_all[me_p] = fit_part[my_part]
-    fit_full[my_part, me_a] = jnp.sum(fit_all[...], axis=0).astype(BF16)
-    fit_gather = [
-        remote(
-            fit_full.at[my_part, me_a],
-            fit_full.at[my_part, me_a],
-            g_send.at[i],
-            g_recv.at[me_a],
-            "aux",
-            peer,
-        )
-        for i, peer in enumerate(aux_peers)
-    ]
-    for copy in fit_gather:
-        copy.start()
+    def red_copy(i, peer):
+        ref = red_all.at[pl.ds(me_p * slots, slots)]
+        return remote(ref, ref, p_send.at[i], p_recv.at[me_p], "pair", peer)
 
     def reduce_chunk():
         total = coul_send[me_a].astype(F32)
@@ -271,56 +283,89 @@
                 coul_recv.at[peer], coul_recv.at[peer], r_send.at[0], r_recv.at[peer], "aux", peer
             ).wait_recv()
             total = total + coul_recv[peer].astype(F32)
-        red_all[me_p] = (total * (1.0 / math.sqrt(total_aux))).astype(BF16)
+        red_all[pl.ds(me_p * slots, slots)] = (total * (1.0 / math.sqrt(total_aux))).astype(BF16)
         for i, peer in enumerate(pair_peers):
-            remote(
-                red_all.at[me_p], red_all.at[me_p], p_send.at[i], p_recv.at[me_p], "pair", peer
-            ).start()
+            red_copy(i, peer).start()
 
     if_reducer(reduce_chunk)
 
-    places = []
-    count = jnp.int32(0)
-    for h in range(n_pair * slots):
-        mine = (owner_s[h] == me_p).astype(jnp.int32) * mask_s[h]
-        count = count + mine
-        places.append(count * mine)
+    for i, peer in enumerate(pair_peers):
+        remote(
+            fit_part.at[0], fit_all.at[peer], f_send.at[i], f_recv.at[peer], "pair", peer
+        ).wait_recv()
+    fit_all[me_p] = fit_part[my_part]
+    fit_full[my_part, me_a] = jnp.sum(fit_all[...], axis=0).astype(BF16)
+
+    neighbour = me_a + 1 - 2 * lax.rem(me_a, 2)
+    evens = [lax.rem(me_a + 2 * i, n_aux) for i in range(1, n_aux // 2)]
+
+    def fit_copy(source, peer, sem):
+        ref = fit_full.at[my_part, source]
+        return remote(ref, ref, g_send.at[sem], g_recv.at[source], "aux", peer)
+
+    def fock_copy(source, peer, sem):
+        return remote(
+            fock_all.at[source], fock_all.at[source], a_send.at[sem], a_recv.at[source], "aux", peer
+        )
+
+    def fan_out(copy):
+        for i, peer in enumerate(evens):
+            copy(me_a, peer, i + 1).start()
+        copy(me_a, neighbour, 0).start()
+
+    fan_out(fit_copy)
 
     def place_chunk():
         for i, peer in enumerate(pair_peers):
             remote(
-                red_all.at[peer], red_all.at[peer], p_send.at[i], p_recv.at[peer], "pair", peer
+                red_all.at[pl.ds(peer * slots, slots)],
+                red_all.at[pl.ds(peer * slots, slots)],
+                p_send.at[i],
+                p_recv.at[peer],
+                "pair",
+                peer,
             ).wait_recv()
         for k in range(owned):
-            block = jnp.zeros((chunk_rows, width), F32)
-            for h in range(k, n_pair * slots):
-                weight = (places[h] == k + 1).astype(F32)
-                block = block + weight * red_all[h // slots, h % slots].astype(F32)
+            block = red_all[place_at[k]].astype(F32) * place_on[k]
             fock_all[me_a, k] = block.astype(BF16)
-        for i, peer in enumerate(aux_peers):
-            remote(
-                fock_all.at[me_a], fock_all.at[me_a], a_send.at[i], a_recv.at[me_a], "aux", peer
-            ).start()
+        fan_out(fock_copy)
+
+    if_reducer(place_chunk)
+
+    for i, source in enumerate(evens):
+        fit_copy(source, neighbour, 0).wait_recv()
+        fit_copy(source, neighbour, n_aux // 2 + i).start()
+
+    def spread_chunk(source):
+        at = pl.multiple_of(source * chunk_rows, chunk_rows)
         for k in range(owned):
-            fock_o[k, pl.ds(pl.multiple_of(me_a * chunk_rows, chunk_rows), chunk_rows), :] = (
-                fock_all[me_a, k].astype(F32)
-            )
-
-    if_reducer(place_chunk)
-
-    for i, peer in enumerate(aux_peers):
-        remote(
-            fit_full.at[my_part, peer],
-            fit_full.at[my_part, peer],
-            g_send.at[i],
-            g_recv.at[peer],
-            "aux",
-            peer,
-        ).wait_recv()
-    to_mate = remote(
-        fit_full.at[my_part], fit_full.at[my_part], m_send, m_recv, "pair", mate
-    )
+            fock_o[k, pl.ds(at, chunk_rows), :] = fock_all[source, k].astype(F32)
+
+    my_side = lax.rem(me_a, 2)
+    if chunks == n_aux:
+        near = [me_a] + evens
+        far = [source + 1 - 2 * my_side for source in near]
+    else:
+        near = [2 * j + my_side for j in range(chunks // 2)]
+        far = [2 * j + 1 - my_side for j in range(chunks // 2)]
+
+    for j, source in enumerate(near):
+
+        def pass_on(source=source, j=j):
+            fock_copy(source, neighbour, 0).wait_recv()
+            fock_copy(source, neighbour, n_aux // 2 + j).start()
+
+        if chunks < n_aux:
+            pl.when(me_a != source)(pass_on)
+        elif j > 0:
+            pass_on()
+
+    for source in [me_a] + evens:
+        fit_copy(source + 1 - 2 * my_side, neighbour, 0).wait_recv()
+    to_mate = remote(fit_full.at[my_part], fit_full.at[my_part], m_send, m_recv, "pair", mate)
     to_mate.start()
+    for source in near:
+        spread_chunk(source)
     remote(
         fit_full.at[1 - my_part], fit_full.at[1 - my_part], m_send, m_recv, "pair", mate
     ).wait_recv()
@@ -330,42 +375,33 @@
     left = lax.dot_general(pick, fitted, NT, preferred_element_type=F32).astype(BF16)
     gram_o[...] = jnp.dot(left, fitted, preferred_element_type=F32) * (1.0 / total_aux)
 
-    def each_source(body):
-        for off in range(chunks):
-            if chunks == n_aux:
-                if off > 0:
-                    body(lax.rem(me_a + off, n_aux))
-            else:
-                pl.when(me_a != off)(functools.partial(body, off))
-
-    def take_chunk(peer):
-        remote(
-            fock_all.at[peer], fock_all.at[peer], a_send.at[0], a_recv.at[peer], "aux", peer
-        ).wait_recv()
-        at = peer * chunk_rows
-        if not isinstance(at, int):
-            at = pl.multiple_of(at, chunk_rows)
-        for k in range(owned):
-            fock_o[k, pl.ds(at, chunk_rows), :] = fock_all[peer, k].astype(F32)
-
-    each_source(take_chunk)
-
-    for copy in coup_copies + fit_copies + fit_gather:
+    for source in far:
+        fock_copy(source, neighbour, 0).wait_recv()
+        spread_chunk(source)
+
+    for copy in coup_copies + fit_copies:
         copy.wait_send()
     to_mate.wait_send()
     each_target(end_chunk)
+    for i in range(n_aux - 1):
+        fit_copy(me_a, neighbour, i).wait_send()
 
     def end_sends():
         for i, peer in enumerate(pair_peers):
-            remote(
-                red_all.at[me_p], red_all.at[me_p], p_send.at[i], p_recv.at[me_p], "pair", peer
-            ).wait_send()
-        for i, peer in enumerate(aux_peers):
-            remote(
-                fock_all.at[me_a], fock_all.at[me_a], a_send.at[i], a_recv.at[me_a], "aux", peer
-            ).wait_send()
+            red_copy(i, peer).wait_send()
+        for i in range(n_aux // 2):
+            fock_copy(me_a, neighbour, i).wait_send()
 
     if_reducer(end_sends)
+    for j, source in enumerate(near):
+
+        def end_pass(source=source, j=j):
+            fock_copy(source, neighbour, n_aux // 2 + j).wait_send()
+
+        if chunks < n_aux:
+            pl.when(me_a != source)(end_pass)
+        elif j > 0:
+            end_pass()
 
 
 def shards(three_centre, block_mask, block_owner, block_index, active_orbitals, inactive_orbitals):
@@ -382,18 +418,21 @@
     part_pad = -(-(rows // parts) // 16) * 16
     owned = n_pair * slots // 2
     dma = pltpu.SemaphoreType.DMA
-    smem = pl.BlockSpec(memory_space=pltpu.SMEM)
     vmem = pl.BlockSpec(memory_space=pltpu.VMEM)
-    anywhere = pl.BlockSpec(memory_space=pl.ANY)
+    hbm = pl.BlockSpec(memory_space=pltpu.HBM)
     return pl.pallas_call(
         functools.partial(kernel, n_aux, n_pair),
         out_shape=(
             jax.ShapeDtypeStruct((owned, width, width), F32),
             jax.ShapeDtypeStruct((pairs // n_aux, pairs), F32),
         ),
-        in_specs=[anywhere, smem, smem, smem, vmem, anywhere],
+        in_specs=[hbm] * 6,
         out_specs=(vmem, vmem),
         scratch_shapes=[
+            pltpu.SMEM(block_mask.shape, jnp.int32),
+            pltpu.SMEM(block_owner.shape, jnp.int32),
+            pltpu.SMEM(block_index.shape, jnp.int32),
+            pltpu.VMEM(active_orbitals.shape, BF16),
             pltpu.VMEM(three_centre.shape, BF16),
             pltpu.VMEM((blocks, inactive_orbitals.shape[0], width), BF16),
             pltpu.VMEM((blocks, act, width), F32),
@@ -407,8 +446,9 @@
             pltpu.VMEM((parts, n_aux, part_pad, pairs), BF16),
             pltpu.VMEM((chunks, slots, chunk_rows, width), BF16),
             pltpu.VMEM((n_aux, slots, chunk_rows, width), BF16),
-            pltpu.VMEM((n_pair, slots, chunk_rows, width), BF16),
+            pltpu.VMEM((n_pair * slots, chunk_rows, width), BF16),
             pltpu.VMEM((chunks, owned, chunk_rows, width), BF16),
+            dma((4,)),
             dma((slots,)),
             dma((blocks,)),
             dma((n_pair,)),
@@ -427,7 +467,7 @@
             dma((chunks,)),
         ],
         compiler_params=pltpu.CompilerParams(
-            collective_id=0, has_side_effects=True, vmem_limit_bytes=48 * 1024 * 1024
+            collective_id=0, has_side_effects=True, vmem_limit_bytes=60 * 1024 * 1024
         ),
     )(
         three_centre,

time: 35.7 us -> 33.2 us (0.930)
  local copies, waits for them, and re-layouts: 7.51 us -> 3.48 us
  Pallas kernels: 27 us -> 28.9 us
    unnamed x14 -> x2, local copies, waits for them, and re-layouts: 7.51 us -> 3.48 us
    pallas_call x1, Pallas kernels: 27 us -> 28.9 us  [shards(): pl.pallas_call(functools.partial(kernel, n_aux, n_pair), out_shape=(jax.S...]
where the time goes in v2:
time: 33.2 us; the launch traced here: 33 us
  Pallas kernels  28.9 us (87%)
  local copies, waits for them, and re-layouts  3.48 us (10%)
  between operations  0.64 us (2%)
    pallas_call x1, Pallas kernels, shards(): pl.pallas_call(functools.partial(kernel, n_aux, n_pair), out_shape=(jax.S...  28.9 us
    unnamed x2, local copies, waits for them, and re-layouts  3.48 us

profile of v2, /device:TPU:0, one launch (start us, length us, event | category | flops | bytes accessed | tf_op | source)
XLA Modules:
  0.0 33.0 jit_solution(1586828912172943043)
XLA Ops:
  0.6 28.9 %shard_map.77 = (f32[8,128,128]{2,1,0:T(8,128)}, f32[72,576]{1,0:T(8,128)}) custom-call(bf16[4,20,128,128]{3,2,1,0:T(8,128)(2,1)} %three_hbm.1, s32[16]{0:T(128)} %mask_hbm.1, s32[16]{0:T(128)} %owner_hbm.1, s32[2,16]{1,0:T(2,128)} %index_hbm.1, bf16[24,3072]{1,0:T(8,128)(2,1)} %act_hbm.1, bf16[256,3072]{1,0:T(8,128)(2,1)} %inact_hbm.1), custom_call_target="tpu_custom_call" | custom-call | tf_op jit(solution)/shard_map/pallas_call | solution.py:423
  29.5 1.9 %copy.10 = f32[8,128,128]{2,1,0:T(8,128)} copy(f32[8,128,128]{2,1,0:T(8,128)} %get-tuple-element.4) | data formatting | bytes 1048576
  31.4 1.6 %copy.11 = f32[72,576]{1,0:T(8,128)} copy(f32[72,576]{1,0:T(8,128)} %get-tuple-element.5) | data formatting | bytes 331776

commit v3 on v2

--- a/solution.py
+++ b/solution.py
@@ -219,17 +219,6 @@
     coupling = jnp.sum(jnp.sum(coup_all[...], axis=0), axis=1, keepdims=True) * (1.0 / width)
     coupling = coupling.astype(BF16).astype(F32)
     coup_rows[...] = jnp.broadcast_to(coupling, coup_rows.shape)
-    for g in range(slots):
-
-        def coulomb_step(i, total, g=g):
-            for j in range(step):
-                p = i * step + j
-                total = total + t_v[g, p].astype(F32) * coup_rows[pl.ds(p, 1), :]
-            return total
-
-        total = lax.fori_loop(0, rows // step, coulomb_step, jnp.zeros((width, width), F32))
-        coul_send[:, g] = total.astype(BF16).reshape(chunks, chunk_rows, width)
-
     def each_target(body):
         for off in range(chunks):
             if chunks == n_aux:
@@ -238,17 +227,33 @@
             else:
                 pl.when(me_a != off)(functools.partial(body, off, off))
 
-    def start_chunk(i, peer):
-        remote(
-            coul_send.at[peer], coul_recv.at[me_a], r_send.at[i], r_recv.at[me_a], "aux", peer
-        ).start()
-
-    def end_chunk(i, peer):
-        remote(
-            coul_send.at[peer], coul_recv.at[me_a], r_send.at[i], r_recv.at[me_a], "aux", peer
-        ).wait_send()
-
-    each_target(start_chunk)
+    def chunk_copy(g, i, peer):
+        return remote(
+            coul_send.at[peer, g],
+            coul_recv.at[me_a, g],
+            r_send.at[g, i],
+            r_recv.at[g, me_a],
+            "aux",
+            peer,
+        )
+
+    def start_chunk(g, i, peer):
+        chunk_copy(g, i, peer).start()
+
+    def end_chunk(g, i, peer):
+        chunk_copy(g, i, peer).wait_send()
+
+    for g in range(slots):
+
+        def coulomb_step(i, total, g=g):
+            for j in range(step):
+                p = i * step + j
+                total = total + t_v[g, p].astype(F32) * coup_rows[pl.ds(p, 1), :]
+            return total
+
+        total = lax.fori_loop(0, rows // step, coulomb_step, jnp.zeros((width, width), F32))
+        coul_send[:, g] = total.astype(BF16).reshape(chunks, chunk_rows, width)
+        each_target(functools.partial(start_chunk, g))
 
     second = lax.rem(lax.broadcasted_iota(jnp.int32, (act_pad, pairs), 1), act)
     keep = (second == lax.broadcasted_iota(jnp.int32, (act_pad, pairs), 0)).astype(F32)
@@ -277,13 +282,13 @@
         return remote(ref, ref, p_send.at[i], p_recv.at[me_p], "pair", peer)
 
     def reduce_chunk():
-        total = coul_send[me_a].astype(F32)
-        for i, peer in enumerate(aux_peers):
-            remote(
-                coul_recv.at[peer], coul_recv.at[peer], r_send.at[0], r_recv.at[peer], "aux", peer
-            ).wait_recv()
-            total = total + coul_recv[peer].astype(F32)
-        red_all[pl.ds(me_p * slots, slots)] = (total * (1.0 / math.sqrt(total_aux))).astype(BF16)
+        for g in range(slots):
+            total = coul_send[me_a, g].astype(F32)
+            for peer in aux_peers:
+                ref = coul_recv.at[peer, g]
+                remote(ref, ref, r_send.at[0, 0], r_recv.at[g, peer], "aux", peer).wait_recv()
+                total = total + coul_recv[peer, g].astype(F32)
+            red_all[me_p * slots + g] = (total * (1.0 / math.sqrt(total_aux))).astype(BF16)
         for i, peer in enumerate(pair_peers):
             red_copy(i, peer).start()
 
@@ -382,7 +387,8 @@
     for copy in coup_copies + fit_copies:
         copy.wait_send()
     to_mate.wait_send()
-    each_target(end_chunk)
+    for g in range(slots):
+        each_target(functools.partial(end_chunk, g))
     for i in range(n_aux - 1):
         fit_copy(me_a, neighbour, i).wait_send()
 
@@ -402,6 +408,18 @@
             pl.when(me_a != source)(end_pass)
         elif j > 0:
             end_pass()
+
+
+def finish(fock_in, gram_in, fock_out, gram_out, sem):
+    owned = fock_in.shape[0]
+    copies = [
+        pltpu.make_async_copy(fock_in.at[k], fock_out.at[k], sem.at[k]) for k in range(owned)
+    ]
+    copies.append(pltpu.make_async_copy(gram_in, gram_out, sem.at[owned]))
+    for copy in copies:
+        copy.start()
+    for copy in copies:
+        copy.wait()
 
 
 def shards(three_centre, block_mask, block_owner, block_index, active_orbitals, inactive_orbitals):
@@ -420,7 +438,7 @@
     dma = pltpu.SemaphoreType.DMA
     vmem = pl.BlockSpec(memory_space=pltpu.VMEM)
     hbm = pl.BlockSpec(memory_space=pltpu.HBM)
-    return pl.pallas_call(
+    fock, gram = pl.pallas_call(
         functools.partial(kernel, n_aux, n_pair),
         out_shape=(
             jax.ShapeDtypeStruct((owned, width, width), F32),
@@ -455,8 +473,8 @@
             dma((n_pair,)),
             dma((n_pair,)),
             dma((n_pair,)),
-            dma((chunks,)),
-            dma((n_aux,)),
+            dma((slots, chunks)),
+            dma((slots, n_aux)),
             dma((n_aux,)),
             dma((n_aux,)),
             dma,
@@ -477,6 +495,17 @@
         active_orbitals,
         inactive_orbitals,
     )
+    return pl.pallas_call(
+        finish,
+        out_shape=(
+            jax.ShapeDtypeStruct(fock.shape, F32),
+            jax.ShapeDtypeStruct(gram.shape, F32),
+        ),
+        in_specs=[hbm, hbm],
+        out_specs=(hbm, hbm),
+        scratch_shapes=[dma((owned + 1,))],
+        compiler_params=pltpu.CompilerParams(vmem_limit_bytes=60 * 1024 * 1024),
+    )(fock, gram)
 
 
 def solution(mesh):

time: 33.2 us -> 52.3 us (1.58)
  Pallas kernels: 28.9 us -> 51.5 us
  local copies, waits for them, and re-layouts: 3.48 us -> 0 us
    pallas_call x0 -> x1, Pallas kernels: none -> 22.6 us  [shards(): pl.pallas_call(finish, out_shape=(jax.ShapeDtypeStruct(fock.shape, F32),...]
    unnamed x2 -> x0, local copies, waits for them, and re-layouts: 3.48 us -> none
where the time goes in v3:
time: 52.3 us; the launch traced here: 52.2 us
  Pallas kernels  51.5 us (98%)
  between operations  0.64 us (1%)
    pallas_call x1, Pallas kernels, shards(): pl.pallas_call(functools.partial(kernel, n_aux, n_pair), out_shape=(jax.S...  28.9 us
    pallas_call x1, Pallas kernels, shards(): pl.pallas_call(finish, out_shape=(jax.ShapeDtypeStruct(fock.shape, F32),...  22.6 us

profile of v3, /device:TPU:0, one launch (start us, length us, event | category | flops | bytes accessed | tf_op | source)
XLA Modules:
  0.0 52.2 jit_solution(17960062710367086237)
XLA Ops:
  0.6 28.9 %shard_map.77 = (f32[8,128,128]{2,1,0:T(8,128)}, f32[72,576]{1,0:T(8,128)}) custom-call(bf16[4,20,128,128]{3,2,1,0:T(8,128)(2,1)} %three_hbm.1, s32[16]{0:T(128)} %mask_hbm.1, s32[16]{0:T(128)} %owner_hbm.1, s32[2,16]{1,0:T(2,128)} %index_hbm.1, bf16[24,3072]{1,0:T(8,128)(2,1)} %act_hbm.1, bf16[256,3072]{1,0:T(8,128)(2,1)} %inact_hbm.1), custom_call_target="tpu_custom_call" | custom-call | tf_op jit(solution)/shard_map/pallas_call | solution.py:441
  29.5 22.6 %shard_map.78 = (f32[8,128,128]{2,1,0:T(8,128)}, f32[72,576]{1,0:T(8,128)}) custom-call(f32[8,128,128]{2,1,0:T(8,128)} %get-tuple-element.4.fock_in, f32[72,576]{1,0:T(8,128)} %get-tuple-element.5.gram_in), custom_call_target="tpu_custom_call" | custom-call | tf_op jit(solution)/shard_map/pallas_call | solution.py:498

commit v4 on v3

--- a/solution.py
+++ b/solution.py
@@ -410,15 +410,18 @@
             end_pass()
 
 
-def finish(fock_in, gram_in, fock_out, gram_out, sem):
+def finish(fock_in, gram_in, fock_out, gram_out, fock_v, gram_v, in_sem, out_sem):
     owned = fock_in.shape[0]
-    copies = [
-        pltpu.make_async_copy(fock_in.at[k], fock_out.at[k], sem.at[k]) for k in range(owned)
-    ]
-    copies.append(pltpu.make_async_copy(gram_in, gram_out, sem.at[owned]))
-    for copy in copies:
+    legs = [(fock_in.at[k], fock_v.at[k], fock_out.at[k]) for k in range(owned)]
+    legs.append((gram_in, gram_v, gram_out))
+    inward = [pltpu.make_async_copy(a, v, in_sem.at[i]) for i, (a, v, _) in enumerate(legs)]
+    outward = [pltpu.make_async_copy(v, b, out_sem.at[i]) for i, (_, v, b) in enumerate(legs)]
+    for copy in inward:
         copy.start()
-    for copy in copies:
+    for arrive, leave in zip(inward, outward):
+        arrive.wait()
+        leave.start()
+    for copy in outward:
         copy.wait()
 
 
@@ -503,7 +506,12 @@
         ),
         in_specs=[hbm, hbm],
         out_specs=(hbm, hbm),
-        scratch_shapes=[dma((owned + 1,))],
+        scratch_shapes=[
+            pltpu.VMEM(fock.shape, F32),
+            pltpu.VMEM(gram.shape, F32),
+            dma((owned + 1,)),
+            dma((owned + 1,)),
+        ],
         compiler_params=pltpu.CompilerParams(vmem_limit_bytes=60 * 1024 * 1024),
     )(fock, gram)
 

time: 52.3 us -> 31.7 us (0.61)
  Pallas kernels: 51.5 us -> 30.9 us
    pallas_call x1, Pallas kernels: 22.6 us -> 2.02 us  [shards(): pl.pallas_call(finish, out_shape=(jax.ShapeDtypeStruct(fock.shape, F32),...]
where the time goes in v4:
time: 31.7 us; the launch traced here: 31.5 us
  Pallas kernels  30.9 us (97%)
  between operations  0.64 us (2%)
    pallas_call x1, Pallas kernels, shards(): pl.pallas_call(functools.partial(kernel, n_aux, n_pair), out_shape=(jax.S...  28.9 us
    pallas_call x1, Pallas kernels, shards(): pl.pallas_call(finish, out_shape=(jax.ShapeDtypeStruct(fock.shape, F32),...  2.02 us

profile of v4, /device:TPU:0, one launch (start us, length us, event | category | flops | bytes accessed | tf_op | source)
XLA Modules:
  0.0 31.5 jit_solution(582853191770054615)
XLA Ops:
  0.6 28.9 %shard_map.77 = (f32[8,128,128]{2,1,0:T(8,128)}, f32[72,576]{1,0:T(8,128)}) custom-call(bf16[4,20,128,128]{3,2,1,0:T(8,128)(2,1)} %three_hbm.1, s32[16]{0:T(128)} %mask_hbm.1, s32[16]{0:T(128)} %owner_hbm.1, s32[2,16]{1,0:T(2,128)} %index_hbm.1, bf16[24,3072]{1,0:T(8,128)(2,1)} %act_hbm.1, bf16[256,3072]{1,0:T(8,128)(2,1)} %inact_hbm.1), custom_call_target="tpu_custom_call" | custom-call | tf_op jit(solution)/shard_map/pallas_call | solution.py:444
  29.5 2.0 %shard_map.78 = (f32[8,128,128]{2,1,0:T(8,128)}, f32[72,576]{1,0:T(8,128)}) custom-call(f32[8,128,128]{2,1,0:T(8,128)} %get-tuple-element.4.fock_in, f32[72,576]{1,0:T(8,128)} %get-tuple-element.5.gram_in), custom_call_target="tpu_custom_call" | custom-call | tf_op jit(solution)/shard_map/pallas_call | solution.py:501
